TPU v7x, 512 devices: a whole 4x8x8 slice. The times are simulated.
512 devices in a mesh: ctx: 32 (over x, y), tp: 16 (over z, core).
Axes of the slice: x: 4, y: 8, z: 8, core: 2. Of those that a mesh axis runs over, the one named last changes fastest.
Arguments:
- prefix_x: bfloat16 [8192, 8192], P('ctx', 'tp'), may hold values from -6 to 6
- prefix_z: bfloat16 [8192, 8192], P('ctx', 'tp'), may hold values from -6 to 6
- prefix_bc: bfloat16 [8192, 256], P(('ctx', 'tp')), may hold values from -6 to 6
- prefix_dt: float32 [128, 8192], P('tp', 'ctx'), may hold values from -6 to 6
- branch_x: bfloat16 [8192, 8192], P('ctx', 'tp'), may hold values from -6 to 6
- branch_z: bfloat16 [8192, 8192], P('ctx', 'tp'), may hold values from -6 to 6
- branch_bc: bfloat16 [8192, 256], P(('ctx', 'tp')), may hold values from -6 to 6
- branch_dt: float32 [128, 8192], P('tp', 'ctx'), may hold values from -6 to 6
- conv_x: bfloat16 [4, 8192], P(None, 'tp'), may hold values from -3 to 3
- conv_bc: bfloat16 [4, 256], replicated, may hold values from -3 to 3
- decay_rate: float32 [128], P('tp'), may hold values from 2.4414063e-05 to 0.03
- skip: float32 [128], P('tp'), may hold values from 0.5 to 1.5
- norm_gain: float32 [8192], P('tp'), may hold values from 0.5 to 1.5
- bound_pos: int32 [8], replicated, may hold values from 0 to 8191
- branch_owner: int32 [64], replicated, may hold values from 0 to 31, as said below
- branch_parent: int32 [64], replicated, may hold values from 0 to 7
- branch_len: int32 [64], replicated, may hold values from 1 to 255, as said below
Outputs:
- prefix_out: bfloat16 [8192, 8192], P('ctx', 'tp')
- branch_out: bfloat16 [8192, 8192], P('ctx', 'tp')
Inputs may be any that keep to these rules, and one draw needn't show every extreme that they name: `branch_owner`: every block index 0 to 31 holds exactly 2 branches. `branch_len`: the branches of one block have lengths that sum to at most 256; in every draw some block's sum is exactly 256, and some branch has exactly 255 rows.
All inputs are finite; a program needn't handle non-finite values.
Results may differ from a plain program's by a relative error of at most 0.0034.
Values may be sent and summed in bfloat16 or wider, within the bound.
No kernel may reach another device: no remote copies, remote signals or barrier semaphores. Data moves between devices by JAX's collectives and lax.ppermute only.
A program may use at most 64 MiB of HBM per device.

v0:
```python
import jax
import jax.numpy as jnp
from jax import lax
from jax.sharding import PartitionSpec as P

NORM_GROUP = 8192
BR_PER = 2
EPSILON = 1e-05


def passed_along(value, axis, steps):
    count = lax.axis_size(axis)
    first, last = (max(0, -steps), min(count, count - steps))
    return lax.ppermute(value, axis, [(source, source + steps) for source in range(first, last)])


def conv_silu(lagged, weights):
    summed = weights[0].astype(jnp.float32)[None, :] * lagged[0].astype(jnp.float32)
    for tap_index in range(1, len(lagged)):
        summed = summed + weights[tap_index].astype(jnp.float32)[None, :] * lagged[
            tap_index
        ].astype(jnp.float32)
    return jax.nn.silu(summed).astype(jnp.bfloat16)


def split_conv(convolved, channels, head_count):
    length = convolved.shape[0]
    state_size = (convolved.shape[1] - channels) // 2
    values = convolved[:, :channels].reshape(length, head_count, channels // head_count)
    return (
        values,
        convolved[:, channels : channels + state_size],
        convolved[:, channels + state_size :],
    )


def decays(raw_steps, rates):
    step_size = jax.nn.softplus(raw_steps)
    log_decay = -rates[:, None] * step_size
    return (step_size, log_decay, jnp.cumsum(log_decay, axis=1))


def intra_block(values, b_rows, c_rows, step_size, cumulative, causal_mask):
    scores = jnp.dot(c_rows, b_rows.T, preferred_element_type=jnp.float32)
    exponent = jnp.where(causal_mask[None], cumulative[:, :, None] - cumulative[:, None, :], 0.0)
    mixing = jnp.where(
        causal_mask[None], scores[None] * jnp.exp(exponent) * step_size[:, None, :], 0.0
    ).astype(jnp.bfloat16)
    return jnp.einsum("hts,shp->thp", mixing, values, preferred_element_type=jnp.float32)


def local_states(values, b_rows, step_size, cumulative, positions):
    length = cumulative.shape[1]
    clipped = jnp.clip(positions, 0, length - 1)
    decay_end = jnp.take(cumulative, clipped, axis=1)
    row_index = jnp.arange(length, dtype=jnp.int32)
    inside = row_index[None, :] <= positions[:, None]
    exponent = jnp.where(inside[:, None, :], decay_end.T[:, :, None] - cumulative[None], 0.0)
    weight = jnp.where(inside[:, None, :], jnp.exp(exponent) * step_size[None], 0.0)
    weighted = (
        jnp.transpose(weight, (0, 2, 1))[:, :, :, None] * values[None].astype(jnp.float32)
    ).astype(jnp.bfloat16)
    return jnp.einsum("jshp,sn->jhpn", weighted, b_rows, preferred_element_type=jnp.float32)


def from_state(c_rows, state, weight):
    result = jnp.einsum(
        "tn,hpn->thp", c_rows.astype(jnp.float32), state, precision=lax.Precision.HIGHEST
    )
    return result * weight.T[:, :, None]


def finish(mixed_out, values, skip, gate_rows, gain):
    length = mixed_out.shape[0]
    mixed_out = mixed_out + skip[None, :, None] * values.astype(jnp.float32)
    gated = mixed_out.reshape(length, -1) * jax.nn.silu(gate_rows.astype(jnp.float32))
    partial_squares = jnp.sum(gated * gated, axis=1, keepdims=True)
    total_squares = lax.psum(partial_squares, "tp")
    factor = lax.rsqrt(total_squares / NORM_GROUP + EPSILON)
    return (gated * factor * gain[None, :]).astype(jnp.bfloat16)


def layout(owner_index, branch_owner, branch_parent, branch_len, length):
    owned = (branch_owner == owner_index).astype(jnp.int32)
    owned_rank = jnp.cumsum(owned) - 1
    owned_lengths = owned * branch_len
    starts = jnp.cumsum(owned_lengths) - owned_lengths
    branch_slot = jnp.arange(BR_PER, dtype=jnp.int32)
    chosen = owned[None, :] * (owned_rank[None, :] == branch_slot[:, None]).astype(jnp.int32)
    segment_length = jnp.sum(chosen * branch_len[None, :], axis=1)
    segment_start = jnp.sum(chosen * starts[None, :], axis=1)
    parents = jnp.sum(chosen * branch_parent[None, :], axis=1)
    row_index = jnp.arange(length, dtype=jnp.int32)
    inside = (
        (row_index[None, :] >= segment_start[:, None])
        & (row_index[None, :] < (segment_start + segment_length)[:, None])
    ).astype(jnp.int32)
    live_count = jnp.sum(inside, axis=0)
    segment = jnp.sum(inside * branch_slot[:, None], axis=0) + BR_PER * (1 - live_count)
    offset = row_index - jnp.sum(inside * segment_start[:, None], axis=0)
    return (segment, offset, live_count > 0, parents)


def branch_block(
    joined_rows,
    gate_rows,
    raw_steps,
    all_states,
    all_tails,
    weights,
    rates,
    skip,
    gain,
    owner_index,
    branch_owner,
    branch_parent,
    branch_len,
):
    length, row_width = joined_rows.shape
    channels = gate_rows.shape[1]
    head_count = rates.shape[0]
    tail_count = weights.shape[0] - 1
    segment, offset, live_rows, parents = layout(
        owner_index, branch_owner, branch_parent, branch_len, length
    )
    seed_states = jnp.take(all_states, parents, axis=0)
    tail_rows = jnp.take(all_tails, parents, axis=0).reshape(-1, row_width).astype(jnp.bfloat16)
    column = jnp.arange(tail_rows.shape[0], dtype=jnp.int32)
    column_segment = column // tail_count
    column_row = column % tail_count
    lagged = []
    for tap_index in range(tail_count + 1):
        shift_rows = tail_count - tap_index
        if shift_rows == 0:
            lagged.append(joined_rows)
        else:
            shifted = jnp.concatenate(
                [
                    jnp.zeros((shift_rows, row_width), jnp.bfloat16),
                    joined_rows[: length - shift_rows],
                ],
                axis=0,
            )
            local_rows = jnp.where(
                (offset >= shift_rows)[:, None], shifted, jnp.zeros_like(shifted)
            )
            picker = (
                (segment[:, None] == column_segment[None, :])
                & (offset[:, None] < shift_rows)
                & (column_row[None, :] == tail_count - shift_rows + offset[:, None])
            ).astype(jnp.bfloat16)
            tail_part = jnp.dot(picker, tail_rows, preferred_element_type=jnp.float32).astype(
                jnp.bfloat16
            )
            lagged.append(local_rows + tail_part)
    values, b_rows, c_rows = split_conv(conv_silu(lagged, weights), channels, head_count)
    step_size, log_decay, cumulative = decays(raw_steps, rates)
    row_index = jnp.arange(length, dtype=jnp.int32)
    causal_mask = (
        (segment[:, None] == segment[None, :])
        & live_rows[:, None]
        & (row_index[None, :] <= row_index[:, None])
    )
    mixed_out = intra_block(values, b_rows, c_rows, step_size, cumulative, causal_mask)
    first_rows = jnp.clip(row_index - offset, 0, length - 1)
    start_log = jnp.take(cumulative - log_decay, first_rows, axis=1)
    seed_weight = jnp.where(
        live_rows[None, :], jnp.exp(jnp.where(live_rows[None, :], cumulative - start_log, 0.0)), 0.0
    )
    for branch_slot in range(seed_states.shape[0]):
        portion = from_state(c_rows, seed_states[branch_slot], seed_weight)
        mixed_out = mixed_out + jnp.where((segment == branch_slot)[:, None, None], portion, 0.0)
    result = finish(mixed_out, values, skip, gate_rows, gain)
    return jnp.where(live_rows[:, None], result, jnp.zeros_like(result))


def body(
    prefix_x,
    prefix_z,
    prefix_bc,
    prefix_dt,
    branch_x,
    branch_z,
    branch_bc,
    branch_dt,
    conv_x,
    conv_bc,
    decay_rate,
    skip,
    norm_gain,
    bound_pos,
    branch_owner,
    branch_parent,
    branch_len,
):
    prefix_gathered, branch_gathered = (
        lax.all_gather(prefix_bc, "tp", axis=0, tiled=True),
        lax.all_gather(branch_bc, "tp", axis=0, tiled=True),
    )
    length = prefix_x.shape[0]
    channels = prefix_x.shape[1]
    head_count = decay_rate.shape[0]
    weights = jnp.concatenate([conv_x, conv_bc], axis=1)
    tail_count = weights.shape[0] - 1
    joined_rows = jnp.concatenate([prefix_x, prefix_gathered], axis=1)
    before = passed_along(joined_rows[length - tail_count :], "ctx", 1)
    extended = jnp.concatenate([before, joined_rows], axis=0)
    lagged = [extended[tap_index : tap_index + length] for tap_index in range(tail_count + 1)]
    values, b_rows, c_rows = split_conv(conv_silu(lagged, weights), channels, head_count)
    step_size, log_decay, cumulative = decays(prefix_dt, decay_rate)
    row_index = jnp.arange(length, dtype=jnp.int32)
    causal_mask = row_index[None, :] <= row_index[:, None]
    mixed_out = intra_block(values, b_rows, c_rows, step_size, cumulative, causal_mask)
    owner_index = lax.axis_index("ctx")
    local_at = jnp.where(bound_pos // length == owner_index, bound_pos - owner_index * length, -1)
    positions = jnp.concatenate([local_at, jnp.full((1,), length - 1, jnp.int32)])
    states = local_states(values, b_rows, step_size, cumulative, positions)
    bound_count = bound_pos.shape[0]
    end_state = states[bound_count]
    end_decay = jnp.exp(cumulative[:, -1])

    def carry_step(unused, state):
        return passed_along(end_decay[:, None, None] * state + end_state, "ctx", 1)

    entering = lax.fori_loop(0, lax.axis_size("ctx") - 1, carry_step, jnp.zeros_like(end_state))
    mixed_out = mixed_out + from_state(c_rows, entering, jnp.exp(cumulative))
    prefix_out = finish(mixed_out, values, skip, prefix_z, norm_gain)
    held_here = local_at >= 0
    decay_at = jnp.exp(jnp.take(cumulative, jnp.clip(local_at, 0, length - 1), axis=1))
    candidate = jnp.where(
        held_here[:, None, None, None],
        decay_at.T[:, :, None, None] * entering[None] + states[:bound_count],
        0.0,
    )
    tail_index = (local_at[:, None] + 1 + jnp.arange(tail_count, dtype=jnp.int32)[None, :]).reshape(
        -1
    )
    held_rows = jnp.repeat(held_here, tail_count)
    picker = (
        (jnp.arange(length + tail_count, dtype=jnp.int32)[None, :] == tail_index[:, None])
        & held_rows[:, None]
    ).astype(jnp.bfloat16)
    tail_rows = jnp.dot(picker, extended, preferred_element_type=jnp.float32).reshape(
        bound_count, tail_count, -1
    )
    all_states, all_tails = lax.psum((candidate, tail_rows), "ctx")
    branch_joined = jnp.concatenate([branch_x, branch_gathered], axis=1)
    branch_out = branch_block(
        branch_joined,
        branch_z,
        branch_dt,
        all_states,
        all_tails,
        weights,
        decay_rate,
        skip,
        norm_gain,
        owner_index,
        branch_owner,
        branch_parent,
        branch_len,
    )
    return (prefix_out, branch_out)


def solution(mesh):
    in_specs = (
        P("ctx", "tp"),
        P("ctx", "tp"),
        P(("ctx", "tp"), None),
        P("tp", "ctx"),
        P("ctx", "tp"),
        P("ctx", "tp"),
        P(("ctx", "tp"), None),
        P("tp", "ctx"),
        P(None, "tp"),
        P(),
        P("tp"),
        P("tp"),
        P("tp"),
        P(),
        P(),
        P(),
        P(),
    )
    out_specs = (P("ctx", "tp"), P("ctx", "tp"))
    return jax.shard_map(body, mesh=mesh, in_specs=in_specs, out_specs=out_specs, check_vma=False)
```

profile of v0, /device:TPU:1, one launch (start us, length us, event | category | flops | bytes accessed | tf_op | source)
XLA Modules:
  0.0 639.3 jit_solution(6690966973142288056)
XLA Ops:
  8.3 25.1 %all_gather.6 = bf16[256,256]{1,0:T(8,128)(2,1)S(1)} all-gather(bf16[16,256]{1,0:T(8,128)(2,1)} %param.21), channel_id=1, replica_groups=mesh['ctx'=32,'tp'=16] {'tp'}, dimensions={0}, use_global_device_ids=true | all-gather | bytes 139264 | tf_op jit(solution)/shard_map/all_gather | solution.py:197
  50.8 14.8 %all_gather.7 = bf16[256,256]{1,0:T(8,128)(2,1)S(1)} all-gather(bf16[16,256]{1,0:T(8,128)(2,1)S(1)} %copy-done.27), channel_id=1, replica_groups=mesh['ctx'=32,'tp'=16] {'tp'}, dimensions={0}, use_global_device_ids=true | all-gather | bytes 139264 | tf_op jit(solution)/shard_map/all_gather | solution.py:198
  74.3 305.5 %while.10 = (s32[]{:T(128)}, f32[8,64,128]{2,1,0:T(8,128)S(1)}, f32[8]{0:T(128)}, f32[8,64,128]{2,1,0:T(8,128)S(1)}, s32[]{:T(128)}) while((s32[]{:T(128)}, f32[8,64,128]{2,1,0:T(8,128)S(1)}, f32[8]{0:T(128)}, f32[8,64,128]{2,1,0:T(8,128)S(1)}, s32[]{:T(128)}) %tuple.49), condition=%wide.region_3.4_spmd, body=%wide.region_2.3_spmd.sunk | while | flops 131074 | bytes 1835141 | solution.py:225
  78.2 5.5 collective-permute-done
  84.4 4.1 collective-permute-start
  88.6 4.6 collective-permute-done
  93.9 4.1 collective-permute-start
  98.0 3.7 collective-permute-done
  102.4 4.1 collective-permute-start
  106.5 3.3 collective-permute-done
  110.5 3.8 collective-permute-start
  114.3 3.3 collective-permute-done
  118.3 4.4 collective-permute-start
  122.8 3.3 collective-permute-done
  126.8 5.3 collective-permute-start
  132.1 3.3 collective-permute-done
  136.1 5.0 collective-permute-start
  141.1 3.3 collective-permute-done
  145.1 5.0 collective-permute-start
  150.2 4.0 collective-permute-done
  154.9 5.5 collective-permute-start
  160.3 5.0 collective-permute-done
  166.1 5.9 collective-permute-start
  172.0 6.0 collective-permute-done
  178.7 5.4 collective-permute-start
  184.0 4.8 collective-permute-done
  189.5 5.1 collective-permute-start
  194.6 3.7 collective-permute-done
  199.0 4.2 collective-permute-start
  203.2 3.3 collective-permute-done
  207.2 5.3 collective-permute-start
  216.5 5.3 collective-permute-start
  221.9 3.3 collective-permute-done
  225.8 5.5 collective-permute-start
  235.3 5.0 collective-permute-start
  240.3 3.3 collective-permute-done
  244.3 5.2 collective-permute-start
  249.5 4.2 collective-permute-done
  254.5 5.3 collective-permute-start
  259.8 5.0 collective-permute-done
  265.5 4.3 collective-permute-start
  269.9 5.6 collective-permute-done
  276.2 4.1 collective-permute-start
  280.4 5.7 collective-permute-done
  286.7 5.1 collective-permute-start
  291.9 5.8 collective-permute-done
  298.4 6.9 %collective-permute-start = (f32[8,64,128]{2,1,0:T(8,128)S(1)}, f32[8,64,128]{2,1,0:T(8,128)S(1)}, u32[]{:S(2)}, u32[]{:S(2)}) collective-permute-start(f32[8,64,128]{2,1,0:T(8,128)S(1)} %multiply_add_fusion.4), channel_id=1, source_target_pairs={{0,16},{16,32},{32,48},{48,64},{64,80},{80,96},{96,112},{112,128},... | collective-permute-start | bytes 786440 | tf_op jit(solution)/shard_map/while/body/eval_jaxpr/ppermute | solution.py:14
  305.3 5.0 collective-permute-done
  311.0 6.1 collective-permute-start
  317.2 3.7 collective-permute-done
  321.5 6.8 %collective-permute-start = (f32[8,64,128]{2,1,0:T(8,128)S(1)}, f32[8,64,128]{2,1,0:T(8,128)S(1)}, u32[]{:S(2)}, u32[]{:S(2)}) collective-permute-start(f32[8,64,128]{2,1,0:T(8,128)S(1)} %multiply_add_fusion.4), channel_id=1, source_target_pairs={{0,16},{16,32},{32,48},{48,64},{64,80},{80,96},{96,112},{112,128},... | collective-permute-start | bytes 786440 | tf_op jit(solution)/shard_map/while/body/eval_jaxpr/ppermute | solution.py:14
  328.4 3.3 collective-permute-done
  332.3 5.0 collective-permute-start
  337.3 3.3 collective-permute-done
  341.3 5.3 collective-permute-start
  346.6 3.3 collective-permute-done
  350.6 5.0 collective-permute-start
  355.7 3.3 collective-permute-done
  359.6 6.1 collective-permute-start
  369.7 6.2 collective-permute-start
  375.9 3.8 collective-permute-done
  385.2 129.7 %psum.29 = bf16[8,3,768]{2,1,0:T(4,128)(2,1)S(1)} all-reduce(f32[8,3,768]{2,1,0:T(4,128)S(1)} %reshape.508), channel_id=1, replica_groups=mesh['ctx'=32,'tp'=16] {'ctx'}, use_global_device_ids=true, to_apply=%region_14.15 | all-reduce | flops 18432 | bytes 110592 | tf_op jit(solution)/shard_map/psum | solution.py:246
  520.7 75.1 %all-reduce.6.cloned.1.call-done = f32[8,8,64,128]{3,2,1,0:T(8,128)} async-done(((f32[8,8,64,128]{3,2,1,0:T(8,128)}), f32[8,8,64,128]{3,2,1,0:T(8,128)}) %all-reduce.6.cloned.1.call-update) | async-done | bytes 2097168 | tf_op jit(solution)/shard_map/psum | solution.py:246
  602.0 28.6 %all-reduce.3 = (f32[256,1]{0,1:T(1,128)S(1)}, f32[256,1]{0,1:T(1,128)S(1)}) all-reduce(f32[256,1]{0,1:T(1,128)S(1)} %bitcast.99, f32[256,1]{0,1:T(1,128)S(1)} %bitcast.102), channel_id=1, replica_groups=mesh['ctx'=32,'tp'=16] {'tp'}, use_global_device_ids=true, to_apply=%region_5.6 | all-reduce | flops 512 | bytes 4096 | tf_op jit(solution)/shard_map/psum | solution.py:78
  (271 shorter events, 80.0 us)
Async XLA Ops:
  7.2 37.2 %copy-start.45 = (s32[64]{0:T(128)S(1)}, s32[64]{0:T(128)}, u32[]{:S(2)}) copy-start(s32[64]{0:T(128)} %param.33) | copy-start | bytes 772
  7.2 37.5 %copy-start.32 = (s32[64]{0:T(128)S(1)}, s32[64]{0:T(128)}, u32[]{:S(2)}) copy-start(s32[64]{0:T(128)} %param.35) | copy-start | bytes 772
  7.2 37.8 %copy-start.55 = (s32[64]{0:T(128)S(1)}, s32[64]{0:T(128)}, u32[]{:S(2)}) copy-start(s32[64]{0:T(128)} %param.34) | copy-start | bytes 772
  7.2 39.3 %copy-start.33 = (bf16[4,512]{1,0:T(4,128)(2,1)S(1)}, bf16[4,512]{1,0:T(4,128)(2,1)}, u32[]{:S(2)}) copy-start(bf16[4,512]{1,0:T(4,128)(2,1)} %param.27) | copy-start | bytes 12292
  7.2 39.3 %copy-start.44 = (bf16[4,256]{1,0:T(4,128)(2,1)S(1)}, bf16[4,256]{1,0:T(4,128)(2,1)}, u32[]{:S(2)}) copy-start(bf16[4,256]{1,0:T(4,128)(2,1)} %param.28) | copy-start | bytes 6148
  7.2 43.6 %copy-start.8 = (bf16[256,512]{1,0:T(8,128)(2,1)S(1)}, bf16[256,512]{1,0:T(8,128)(2,1)}, u32[]{:S(2)}) copy-start(bf16[256,512]{1,0:T(8,128)(2,1)} %param.23) | copy-start | bytes 786436
  7.2 588.5 %all-reduce.6.cloned.1.call-start = ((), (), s32[]{:S(2)}) async-start(), calls=%async_computation | async-start | bytes 4194304 | tf_op jit(solution)/shard_map/psum | solution.py:246
  8.3 42.5 %copy-start.27 = (bf16[16,256]{1,0:T(8,128)(2,1)S(1)}, bf16[16,256]{1,0:T(8,128)(2,1)}, u32[]{:S(2)}) copy-start(bf16[16,256]{1,0:T(8,128)(2,1)} %param.25) | copy-start | bytes 24580
  33.4 38.7 %copy-start.2 = (bf16[256,768]{1,0:T(8,128)(2,1)}, bf16[256,768]{1,0:T(8,128)(2,1)S(1)}, u32[]{:S(2)}) copy-start(bf16[256,768]{1,0:T(8,128)(2,1)S(1)} %constant_dynamic-update-slice_fusion.2) | copy-start | bytes 1179652
  33.5 38.7 %collective-permute-start.1 = (bf16[3,768]{1,0:T(4,128)(2,1)S(1)}, bf16[3,768]{1,0:T(4,128)(2,1)S(1)}, u32[]{:S(2)}, u32[]{:S(2)}) collective-permute-start(bf16[3,768]{1,0:T(4,128)(2,1)S(1)} %slice.119), channel_id=1, source_target_pairs={{0,16},{16,32},{32,48},{48,64},{64,80},{80,96},{96,112},{112,128},... | collective-permute-start | bytes 13832 | tf_op jit(solution)/shard_map/ppermute | solution.py:14
  75.0 8.8 %collective-permute-start = (f32[8,64,128]{2,1,0:T(8,128)S(1)}, f32[8,64,128]{2,1,0:T(8,128)S(1)}, u32[]{:S(2)}, u32[]{:S(2)}) collective-permute-start(f32[8,64,128]{2,1,0:T(8,128)S(1)} %multiply_add_fusion.4), channel_id=1, source_target_pairs={{0,16},{16,32},{32,48},{48,64},{64,80},{80,96},{96,112},{112,128},... | collective-permute-start | bytes 786440 | tf_op jit(solution)/shard_map/while/body/eval_jaxpr/ppermute | solution.py:14
  84.4 8.7 %collective-permute-start = (f32[8,64,128]{2,1,0:T(8,128)S(1)}, f32[8,64,128]{2,1,0:T(8,128)S(1)}, u32[]{:S(2)}, u32[]{:S(2)}) collective-permute-start(f32[8,64,128]{2,1,0:T(8,128)S(1)} %multiply_add_fusion.4), channel_id=1, source_target_pairs={{0,16},{16,32},{32,48},{48,64},{64,80},{80,96},{96,112},{112,128},... | collective-permute-start | bytes 786440 | tf_op jit(solution)/shard_map/while/body/eval_jaxpr/ppermute | solution.py:14
  93.9 7.8 %collective-permute-start = (f32[8,64,128]{2,1,0:T(8,128)S(1)}, f32[8,64,128]{2,1,0:T(8,128)S(1)}, u32[]{:S(2)}, u32[]{:S(2)}) collective-permute-start(f32[8,64,128]{2,1,0:T(8,128)S(1)} %multiply_add_fusion.4), channel_id=1, source_target_pairs={{0,16},{16,32},{32,48},{48,64},{64,80},{80,96},{96,112},{112,128},... | collective-permute-start | bytes 786440 | tf_op jit(solution)/shard_map/while/body/eval_jaxpr/ppermute | solution.py:14
  102.4 7.4 %collective-permute-start = (f32[8,64,128]{2,1,0:T(8,128)S(1)}, f32[8,64,128]{2,1,0:T(8,128)S(1)}, u32[]{:S(2)}, u32[]{:S(2)}) collective-permute-start(f32[8,64,128]{2,1,0:T(8,128)S(1)} %multiply_add_fusion.4), channel_id=1, source_target_pairs={{0,16},{16,32},{32,48},{48,64},{64,80},{80,96},{96,112},{112,128},... | collective-permute-start | bytes 786440 | tf_op jit(solution)/shard_map/while/body/eval_jaxpr/ppermute | solution.py:14
  110.5 7.1 %collective-permute-start = (f32[8,64,128]{2,1,0:T(8,128)S(1)}, f32[8,64,128]{2,1,0:T(8,128)S(1)}, u32[]{:S(2)}, u32[]{:S(2)}) collective-permute-start(f32[8,64,128]{2,1,0:T(8,128)S(1)} %multiply_add_fusion.4), channel_id=1, source_target_pairs={{0,16},{16,32},{32,48},{48,64},{64,80},{80,96},{96,112},{112,128},... | collective-permute-start | bytes 786440 | tf_op jit(solution)/shard_map/while/body/eval_jaxpr/ppermute | solution.py:14
  118.3 7.7 %collective-permute-start = (f32[8,64,128]{2,1,0:T(8,128)S(1)}, f32[8,64,128]{2,1,0:T(8,128)S(1)}, u32[]{:S(2)}, u32[]{:S(2)}) collective-permute-start(f32[8,64,128]{2,1,0:T(8,128)S(1)} %multiply_add_fusion.4), channel_id=1, source_target_pairs={{0,16},{16,32},{32,48},{48,64},{64,80},{80,96},{96,112},{112,128},... | collective-permute-start | bytes 786440 | tf_op jit(solution)/shard_map/while/body/eval_jaxpr/ppermute | solution.py:14
  126.8 8.6 %collective-permute-start = (f32[8,64,128]{2,1,0:T(8,128)S(1)}, f32[8,64,128]{2,1,0:T(8,128)S(1)}, u32[]{:S(2)}, u32[]{:S(2)}) collective-permute-start(f32[8,64,128]{2,1,0:T(8,128)S(1)} %multiply_add_fusion.4), channel_id=1, source_target_pairs={{0,16},{16,32},{32,48},{48,64},{64,80},{80,96},{96,112},{112,128},... | collective-permute-start | bytes 786440 | tf_op jit(solution)/shard_map/while/body/eval_jaxpr/ppermute | solution.py:14
  136.1 8.3 %collective-permute-start = (f32[8,64,128]{2,1,0:T(8,128)S(1)}, f32[8,64,128]{2,1,0:T(8,128)S(1)}, u32[]{:S(2)}, u32[]{:S(2)}) collective-permute-start(f32[8,64,128]{2,1,0:T(8,128)S(1)} %multiply_add_fusion.4), channel_id=1, source_target_pairs={{0,16},{16,32},{32,48},{48,64},{64,80},{80,96},{96,112},{112,128},... | collective-permute-start | bytes 786440 | tf_op jit(solution)/shard_map/while/body/eval_jaxpr/ppermute | solution.py:14
  145.1 9.1 %collective-permute-start = (f32[8,64,128]{2,1,0:T(8,128)S(1)}, f32[8,64,128]{2,1,0:T(8,128)S(1)}, u32[]{:S(2)}, u32[]{:S(2)}) collective-permute-start(f32[8,64,128]{2,1,0:T(8,128)S(1)} %multiply_add_fusion.4), channel_id=1, source_target_pairs={{0,16},{16,32},{32,48},{48,64},{64,80},{80,96},{96,112},{112,128},... | collective-permute-start | bytes 786440 | tf_op jit(solution)/shard_map/while/body/eval_jaxpr/ppermute | solution.py:14
  154.9 10.5 %collective-permute-start = (f32[8,64,128]{2,1,0:T(8,128)S(1)}, f32[8,64,128]{2,1,0:T(8,128)S(1)}, u32[]{:S(2)}, u32[]{:S(2)}) collective-permute-start(f32[8,64,128]{2,1,0:T(8,128)S(1)} %multiply_add_fusion.4), channel_id=1, source_target_pairs={{0,16},{16,32},{32,48},{48,64},{64,80},{80,96},{96,112},{112,128},... | collective-permute-start | bytes 786440 | tf_op jit(solution)/shard_map/while/body/eval_jaxpr/ppermute | solution.py:14
  166.1 11.9 %collective-permute-start = (f32[8,64,128]{2,1,0:T(8,128)S(1)}, f32[8,64,128]{2,1,0:T(8,128)S(1)}, u32[]{:S(2)}, u32[]{:S(2)}) collective-permute-start(f32[8,64,128]{2,1,0:T(8,128)S(1)} %multiply_add_fusion.4), channel_id=1, source_target_pairs={{0,16},{16,32},{32,48},{48,64},{64,80},{80,96},{96,112},{112,128},... | collective-permute-start | bytes 786440 | tf_op jit(solution)/shard_map/while/body/eval_jaxpr/ppermute | solution.py:14
  178.7 10.1 %collective-permute-start = (f32[8,64,128]{2,1,0:T(8,128)S(1)}, f32[8,64,128]{2,1,0:T(8,128)S(1)}, u32[]{:S(2)}, u32[]{:S(2)}) collective-permute-start(f32[8,64,128]{2,1,0:T(8,128)S(1)} %multiply_add_fusion.4), channel_id=1, source_target_pairs={{0,16},{16,32},{32,48},{48,64},{64,80},{80,96},{96,112},{112,128},... | collective-permute-start | bytes 786440 | tf_op jit(solution)/shard_map/while/body/eval_jaxpr/ppermute | solution.py:14
  189.5 8.8 %collective-permute-start = (f32[8,64,128]{2,1,0:T(8,128)S(1)}, f32[8,64,128]{2,1,0:T(8,128)S(1)}, u32[]{:S(2)}, u32[]{:S(2)}) collective-permute-start(f32[8,64,128]{2,1,0:T(8,128)S(1)} %multiply_add_fusion.4), channel_id=1, source_target_pairs={{0,16},{16,32},{32,48},{48,64},{64,80},{80,96},{96,112},{112,128},... | collective-permute-start | bytes 786440 | tf_op jit(solution)/shard_map/while/body/eval_jaxpr/ppermute | solution.py:14
  199.0 7.5 %collective-permute-start = (f32[8,64,128]{2,1,0:T(8,128)S(1)}, f32[8,64,128]{2,1,0:T(8,128)S(1)}, u32[]{:S(2)}, u32[]{:S(2)}) collective-permute-start(f32[8,64,128]{2,1,0:T(8,128)S(1)} %multiply_add_fusion.4), channel_id=1, source_target_pairs={{0,16},{16,32},{32,48},{48,64},{64,80},{80,96},{96,112},{112,128},... | collective-permute-start | bytes 786440 | tf_op jit(solution)/shard_map/while/body/eval_jaxpr/ppermute | solution.py:14
  207.2 8.6 %collective-permute-start = (f32[8,64,128]{2,1,0:T(8,128)S(1)}, f32[8,64,128]{2,1,0:T(8,128)S(1)}, u32[]{:S(2)}, u32[]{:S(2)}) collective-permute-start(f32[8,64,128]{2,1,0:T(8,128)S(1)} %multiply_add_fusion.4), channel_id=1, source_target_pairs={{0,16},{16,32},{32,48},{48,64},{64,80},{80,96},{96,112},{112,128},... | collective-permute-start | bytes 786440 | tf_op jit(solution)/shard_map/while/body/eval_jaxpr/ppermute | solution.py:14
  216.5 8.6 %collective-permute-start = (f32[8,64,128]{2,1,0:T(8,128)S(1)}, f32[8,64,128]{2,1,0:T(8,128)S(1)}, u32[]{:S(2)}, u32[]{:S(2)}) collective-permute-start(f32[8,64,128]{2,1,0:T(8,128)S(1)} %multiply_add_fusion.4), channel_id=1, source_target_pairs={{0,16},{16,32},{32,48},{48,64},{64,80},{80,96},{96,112},{112,128},... | collective-permute-start | bytes 786440 | tf_op jit(solution)/shard_map/while/body/eval_jaxpr/ppermute | solution.py:14
  225.8 8.8 %collective-permute-start = (f32[8,64,128]{2,1,0:T(8,128)S(1)}, f32[8,64,128]{2,1,0:T(8,128)S(1)}, u32[]{:S(2)}, u32[]{:S(2)}) collective-permute-start(f32[8,64,128]{2,1,0:T(8,128)S(1)} %multiply_add_fusion.4), channel_id=1, source_target_pairs={{0,16},{16,32},{32,48},{48,64},{64,80},{80,96},{96,112},{112,128},... | collective-permute-start | bytes 786440 | tf_op jit(solution)/shard_map/while/body/eval_jaxpr/ppermute | solution.py:14
  235.3 8.3 %collective-permute-start = (f32[8,64,128]{2,1,0:T(8,128)S(1)}, f32[8,64,128]{2,1,0:T(8,128)S(1)}, u32[]{:S(2)}, u32[]{:S(2)}) collective-permute-start(f32[8,64,128]{2,1,0:T(8,128)S(1)} %multiply_add_fusion.4), channel_id=1, source_target_pairs={{0,16},{16,32},{32,48},{48,64},{64,80},{80,96},{96,112},{112,128},... | collective-permute-start | bytes 786440 | tf_op jit(solution)/shard_map/while/body/eval_jaxpr/ppermute | solution.py:14
  244.3 9.4 %collective-permute-start = (f32[8,64,128]{2,1,0:T(8,128)S(1)}, f32[8,64,128]{2,1,0:T(8,128)S(1)}, u32[]{:S(2)}, u32[]{:S(2)}) collective-permute-start(f32[8,64,128]{2,1,0:T(8,128)S(1)} %multiply_add_fusion.4), channel_id=1, source_target_pairs={{0,16},{16,32},{32,48},{48,64},{64,80},{80,96},{96,112},{112,128},... | collective-permute-start | bytes 786440 | tf_op jit(solution)/shard_map/while/body/eval_jaxpr/ppermute | solution.py:14
  254.5 10.4 %collective-permute-start = (f32[8,64,128]{2,1,0:T(8,128)S(1)}, f32[8,64,128]{2,1,0:T(8,128)S(1)}, u32[]{:S(2)}, u32[]{:S(2)}) collective-permute-start(f32[8,64,128]{2,1,0:T(8,128)S(1)} %multiply_add_fusion.4), channel_id=1, source_target_pairs={{0,16},{16,32},{32,48},{48,64},{64,80},{80,96},{96,112},{112,128},... | collective-permute-start | bytes 786440 | tf_op jit(solution)/shard_map/while/body/eval_jaxpr/ppermute | solution.py:14
  265.5 10.0 %collective-permute-start = (f32[8,64,128]{2,1,0:T(8,128)S(1)}, f32[8,64,128]{2,1,0:T(8,128)S(1)}, u32[]{:S(2)}, u32[]{:S(2)}) collective-permute-start(f32[8,64,128]{2,1,0:T(8,128)S(1)} %multiply_add_fusion.4), channel_id=1, source_target_pairs={{0,16},{16,32},{32,48},{48,64},{64,80},{80,96},{96,112},{112,128},... | collective-permute-start | bytes 786440 | tf_op jit(solution)/shard_map/while/body/eval_jaxpr/ppermute | solution.py:14
  276.2 9.8 %collective-permute-start = (f32[8,64,128]{2,1,0:T(8,128)S(1)}, f32[8,64,128]{2,1,0:T(8,128)S(1)}, u32[]{:S(2)}, u32[]{:S(2)}) collective-permute-start(f32[8,64,128]{2,1,0:T(8,128)S(1)} %multiply_add_fusion.4), channel_id=1, source_target_pairs={{0,16},{16,32},{32,48},{48,64},{64,80},{80,96},{96,112},{112,128},... | collective-permute-start | bytes 786440 | tf_op jit(solution)/shard_map/while/body/eval_jaxpr/ppermute | solution.py:14
  286.7 11.0 %collective-permute-start = (f32[8,64,128]{2,1,0:T(8,128)S(1)}, f32[8,64,128]{2,1,0:T(8,128)S(1)}, u32[]{:S(2)}, u32[]{:S(2)}) collective-permute-start(f32[8,64,128]{2,1,0:T(8,128)S(1)} %multiply_add_fusion.4), channel_id=1, source_target_pairs={{0,16},{16,32},{32,48},{48,64},{64,80},{80,96},{96,112},{112,128},... | collective-permute-start | bytes 786440 | tf_op jit(solution)/shard_map/while/body/eval_jaxpr/ppermute | solution.py:14
  298.4 11.9 %collective-permute-start = (f32[8,64,128]{2,1,0:T(8,128)S(1)}, f32[8,64,128]{2,1,0:T(8,128)S(1)}, u32[]{:S(2)}, u32[]{:S(2)}) collective-permute-start(f32[8,64,128]{2,1,0:T(8,128)S(1)} %multiply_add_fusion.4), channel_id=1, source_target_pairs={{0,16},{16,32},{32,48},{48,64},{64,80},{80,96},{96,112},{112,128},... | collective-permute-start | bytes 786440 | tf_op jit(solution)/shard_map/while/body/eval_jaxpr/ppermute | solution.py:14
  311.0 9.8 %collective-permute-start = (f32[8,64,128]{2,1,0:T(8,128)S(1)}, f32[8,64,128]{2,1,0:T(8,128)S(1)}, u32[]{:S(2)}, u32[]{:S(2)}) collective-permute-start(f32[8,64,128]{2,1,0:T(8,128)S(1)} %multiply_add_fusion.4), channel_id=1, source_target_pairs={{0,16},{16,32},{32,48},{48,64},{64,80},{80,96},{96,112},{112,128},... | collective-permute-start | bytes 786440 | tf_op jit(solution)/shard_map/while/body/eval_jaxpr/ppermute | solution.py:14
  321.5 10.1 %collective-permute-start = (f32[8,64,128]{2,1,0:T(8,128)S(1)}, f32[8,64,128]{2,1,0:T(8,128)S(1)}, u32[]{:S(2)}, u32[]{:S(2)}) collective-permute-start(f32[8,64,128]{2,1,0:T(8,128)S(1)} %multiply_add_fusion.4), channel_id=1, source_target_pairs={{0,16},{16,32},{32,48},{48,64},{64,80},{80,96},{96,112},{112,128},... | collective-permute-start | bytes 786440 | tf_op jit(solution)/shard_map/while/body/eval_jaxpr/ppermute | solution.py:14
  332.3 8.2 %collective-permute-start = (f32[8,64,128]{2,1,0:T(8,128)S(1)}, f32[8,64,128]{2,1,0:T(8,128)S(1)}, u32[]{:S(2)}, u32[]{:S(2)}) collective-permute-start(f32[8,64,128]{2,1,0:T(8,128)S(1)} %multiply_add_fusion.4), channel_id=1, source_target_pairs={{0,16},{16,32},{32,48},{48,64},{64,80},{80,96},{96,112},{112,128},... | collective-permute-start | bytes 786440 | tf_op jit(solution)/shard_map/while/body/eval_jaxpr/ppermute | solution.py:14
  341.3 8.6 %collective-permute-start = (f32[8,64,128]{2,1,0:T(8,128)S(1)}, f32[8,64,128]{2,1,0:T(8,128)S(1)}, u32[]{:S(2)}, u32[]{:S(2)}) collective-permute-start(f32[8,64,128]{2,1,0:T(8,128)S(1)} %multiply_add_fusion.4), channel_id=1, source_target_pairs={{0,16},{16,32},{32,48},{48,64},{64,80},{80,96},{96,112},{112,128},... | collective-permute-start | bytes 786440 | tf_op jit(solution)/shard_map/while/body/eval_jaxpr/ppermute | solution.py:14
  350.6 8.3 %collective-permute-start = (f32[8,64,128]{2,1,0:T(8,128)S(1)}, f32[8,64,128]{2,1,0:T(8,128)S(1)}, u32[]{:S(2)}, u32[]{:S(2)}) collective-permute-start(f32[8,64,128]{2,1,0:T(8,128)S(1)} %multiply_add_fusion.4), channel_id=1, source_target_pairs={{0,16},{16,32},{32,48},{48,64},{64,80},{80,96},{96,112},{112,128},... | collective-permute-start | bytes 786440 | tf_op jit(solution)/shard_map/while/body/eval_jaxpr/ppermute | solution.py:14
  359.6 9.4 %collective-permute-start = (f32[8,64,128]{2,1,0:T(8,128)S(1)}, f32[8,64,128]{2,1,0:T(8,128)S(1)}, u32[]{:S(2)}, u32[]{:S(2)}) collective-permute-start(f32[8,64,128]{2,1,0:T(8,128)S(1)} %multiply_add_fusion.4), channel_id=1, source_target_pairs={{0,16},{16,32},{32,48},{48,64},{64,80},{80,96},{96,112},{112,128},... | collective-permute-start | bytes 786440 | tf_op jit(solution)/shard_map/while/body/eval_jaxpr/ppermute | solution.py:14
  369.7 10.0 %collective-permute-start = (f32[8,64,128]{2,1,0:T(8,128)S(1)}, f32[8,64,128]{2,1,0:T(8,128)S(1)}, u32[]{:S(2)}, u32[]{:S(2)}) collective-permute-start(f32[8,64,128]{2,1,0:T(8,128)S(1)} %multiply_add_fusion.4), channel_id=1, source_target_pairs={{0,16},{16,32},{32,48},{48,64},{64,80},{80,96},{96,112},{112,128},... | collective-permute-start | bytes 786440 | tf_op jit(solution)/shard_map/while/body/eval_jaxpr/ppermute | solution.py:14
  383.7 131.9 %copy-start.14 = (f32[768]{0:T(1024)S(1)}, f32[768]{0:T(1024)}, u32[]{:S(2)}) copy-start(f32[768]{0:T(1024)} %copy-done.13) | copy-start | bytes 9220
  383.7 131.9 %copy-start.19 = (s32[256]{0:T(256)S(1)}, s32[256]{0:T(256)}, u32[]{:S(2)}) copy-start(s32[256]{0:T(256)} %copy-done.18) | copy-start | bytes 3076
  383.7 131.9 %copy-start.35 = (s32[256]{0:T(256)S(1)}, s32[256]{0:T(256)}, u32[]{:S(2)}) copy-start(s32[256]{0:T(256)} %get-tuple-element.66) | copy-start | bytes 3076
  383.8 131.9 %copy-start.36 = (s32[6]{0:T(128)S(1)}, s32[6]{0:T(128)}, u32[]{:S(2)}) copy-start(s32[6]{0:T(128)} %get-tuple-element.73) | copy-start | bytes 76
  383.8 131.9 %copy-start.37 = (s32[6]{0:T(128)S(1)}, s32[6]{0:T(128)}, u32[]{:S(2)}) copy-start(s32[6]{0:T(128)} %get-tuple-element.74) | copy-start | bytes 76
  383.8 131.9 %copy-start.38 = (pred[6]{0:T(512)(128)(4,1)S(1)}, pred[6]{0:T(512)(128)(4,1)}, u32[]{:S(2)}) copy-start(pred[6]{0:T(512)(128)(4,1)} %broadcast_in_dim.287) | copy-start | bytes 22
  383.8 131.9 %copy-start.41 = (pred[256]{0:T(512)(128)(4,1)S(1)}, pred[256]{0:T(512)(128)(4,1)}, u32[]{:S(2)}) copy-start(pred[256]{0:T(512)(128)(4,1)} %get-tuple-element.61) | copy-start | bytes 772
  383.8 131.9 %copy-start.42 = (pred[256]{0:T(512)(128)(4,1)S(1)}, pred[256]{0:T(512)(128)(4,1)}, u32[]{:S(2)}) copy-start(pred[256]{0:T(512)(128)(4,1)} %get-tuple-element.62) | copy-start | bytes 772
  384.6 131.6 %copy-start.12 = (f32[768]{0:T(1024)S(1)}, f32[768]{0:T(1024)}, u32[]{:S(2)}) copy-start(f32[768]{0:T(1024)} %copy-done.11) | copy-start | bytes 9220
  384.6 131.6 %copy-start.34 = (s32[256]{0:T(256)S(1)}, s32[256]{0:T(256)}, u32[]{:S(2)}) copy-start(s32[256]{0:T(256)} %get-tuple-element.65) | copy-start | bytes 3076
  384.6 131.6 %copy-start.39 = (pred[256]{0:T(512)(128)(4,1)S(1)}, pred[256]{0:T(512)(128)(4,1)}, u32[]{:S(2)}) copy-start(pred[256]{0:T(512)(128)(4,1)} %get-tuple-element.59) | copy-start | bytes 772
  384.6 131.6 %copy-start.40 = (pred[256]{0:T(512)(128)(4,1)S(1)}, pred[256]{0:T(512)(128)(4,1)}, u32[]{:S(2)}) copy-start(pred[256]{0:T(512)(128)(4,1)} %get-tuple-element.60) | copy-start | bytes 772
  384.6 132.0 %copy-start.21 = (f32[768]{0:T(1024)S(1)}, f32[768]{0:T(1024)}, u32[]{:S(2)}) copy-start(f32[768]{0:T(1024)} %copy-done.20) | copy-start | bytes 9220
  384.6 132.0 %copy-start.23 = (f32[768]{0:T(1024)S(1)}, f32[768]{0:T(1024)}, u32[]{:S(2)}) copy-start(f32[768]{0:T(1024)} %copy-done.22) | copy-start | bytes 9220
  384.6 132.0 %copy-start.47 = (s32[256]{0:T(256)S(1)}, s32[256]{0:T(256)}, u32[]{:S(2)}) copy-start(s32[256]{0:T(256)} %get-tuple-element.64) | copy-start | bytes 3076
  384.7 132.0 %copy-start.52 = (pred[256]{0:T(512)(128)(4,1)S(1)}, pred[256]{0:T(512)(128)(4,1)}, u32[]{:S(2)}) copy-start(pred[256]{0:T(512)(128)(4,1)} %get-tuple-element.57) | copy-start | bytes 772
  384.7 132.0 %copy-start.53 = (pred[256]{0:T(512)(128)(4,1)S(1)}, pred[256]{0:T(512)(128)(4,1)}, u32[]{:S(2)}) copy-start(pred[256]{0:T(512)(128)(4,1)} %get-tuple-element.58) | copy-start | bytes 772
  518.2 79.9 %copy-start.49 = (pred[2]{0:T(512)(128)(4,1)S(1)}, pred[2]{0:T(512)(128)(4,1)}, u32[]{:S(2)}) copy-start(pred[2]{0:T(512)(128)(4,1)} %copy-done.48) | copy-start | bytes 10
  518.2 80.0 %copy-start.50 = (pred[256]{0:T(512)(128)(4,1)S(1)}, pred[256]{0:T(512)(128)(4,1)}, u32[]{:S(2)}) copy-start(pred[256]{0:T(512)(128)(4,1)} %broadcast_compare_fusion.2) | copy-start | bytes 772
  519.3 80.1 %copy-start.43 = (pred[256]{0:T(512)(128)(4,1)S(1)}, pred[256]{0:T(512)(128)(4,1)}, u32[]{:S(2)}) copy-start(pred[256]{0:T(512)(128)(4,1)} %get-tuple-element.45) | copy-start | bytes 772
  519.6 81.1 %copy-start.10 = (pred[256,256]{1,0:T(8,128)(4,1)S(1)}, pred[256,256]{1,0:T(8,128)(4,1)}, u32[]{:S(2)}) copy-start(pred[256,256]{1,0:T(8,128)(4,1)} %and_and_fusion) | copy-start | bytes 196612
  519.6 81.1 %copy-start.17 = (f32[8,256]{1,0:T(8,128)S(1)}, f32[8,256]{1,0:T(8,128)}, u32[]{:S(2)}) copy-start(f32[8,256]{1,0:T(8,128)} %copy-done.16) | copy-start | bytes 24580
  519.6 81.1 %copy-start.28 = (f32[8,256]{1,0:T(8,128)S(1)}, f32[8,256]{1,0:T(8,128)}, u32[]{:S(2)}) copy-start(f32[8,256]{1,0:T(8,128)} %copy.135) | copy-start | bytes 24580
  (27 other events, 315.9 us)
Sparse Core Ops, SparseCore 0:
  382.3 213.4 all-reduce.5
where the time goes:
time: 641 us; the launch traced here: 639 us
  waiting for transfers between devices  200 us (31%)
  blocking collectives  198 us (31%)
  starting transfers between devices  161 us (25%)
  other arithmetic  38.4 us (6%)
  local copies, waits for them, and re-layouts  16.2 us (3%)
  between operations  15.2 us (2%)
  matrix products  9.01 us (1%)
    ppermute x32, starting transfers between devices, passed_along(): lax.ppermute(value, axis, [(source, source + steps) for source in range(f...  161 us
    psum x1, blocking collectives, body(): all_states, all_tails = lax.psum((candidate, tail_rows), 'ctx')  130 us
    ppermute x32, waiting for transfers between devices, passed_along(): lax.ppermute(value, axis, [(source, source + steps) for source in range(f...  125 us
    psum x1, waiting for transfers between devices, body(): all_states, all_tails = lax.psum((candidate, tail_rows), 'ctx')  75.1 us
    psum x1, blocking collectives, finish(): total_squares = lax.psum(partial_squares, 'tp')  28.6 us
    all_gather x1, blocking collectives, body(): lax.all_gather(prefix_bc, 'tp', axis=0, tiled=True)  25.1 us
    add x31, other arithmetic, carry_step(): return passed_along(end_decay[:, None, None] * state + end_state, 'ctx', 1)  21.6 us
    all_gather x1, blocking collectives, body(): lax.all_gather(branch_bc, 'tp', axis=0, tiled=True)  14.8 us
  transfers between devices with their start and end apart: 33, of which 32 were waited for; matrix products, arithmetic and copies ran while one was open for 4% of the time, Pallas kernels for 0%

commit v1 on v0

--- a/solution.py
+++ b/solution.py
@@ -194,7 +194,9 @@
     branch_len,
 ):
     prefix_gathered, branch_gathered = (
-        lax.all_gather(prefix_bc, "tp", axis=0, tiled=True),
+        jnp.concatenate(
+            lax.all_to_all(jnp.stack([prefix_bc] * lax.axis_size("tp")), "tp", 0, 0), axis=0
+        ),
         lax.all_gather(branch_bc, "tp", axis=0, tiled=True),
     )
     length = prefix_x.shape[0]

time: 641 us -> 637 us (level)
  blocking collectives: 198 us -> 176 us
  starting transfers between devices: 161 us -> 173 us
    all_gather x1 -> x0, blocking collectives: 25.1 us -> none  [body(): lax.all_gather(prefix_bc, 'tp', axis=0, tiled=True)]
    all_to_all x0 -> x1, starting transfers between devices: none -> 11.8 us  [body(): lax.all_to_all(jnp.stack([prefix_bc] * lax.axis_size('tp')), 'tp', 0, 0)]
  transfers between devices with their start and end apart: 33 -> 34, of which waited for: 32 -> 32; matrix products, arithmetic and copies ran while one was open for 4% -> 5% of each run, Pallas kernels for 0% -> 0%
where the time goes in v1:
time: 637 us; the launch traced here: 635 us
  waiting for transfers between devices  202 us (32%)
  blocking collectives  176 us (28%)
  starting transfers between devices  173 us (27%)
  other arithmetic  40.7 us (6%)
  local copies, waits for them, and re-layouts  17.2 us (3%)
  between operations  15.2 us (2%)
  matrix products  9.87 us (2%)
    ppermute x32, starting transfers between devices, passed_along(): lax.ppermute(value, axis, [(source, source + steps) for source in range(f...  161 us
    psum x1, blocking collectives, body(): all_states, all_tails = lax.psum((candidate, tail_rows), 'ctx')  130 us
    ppermute x32, waiting for transfers between devices, passed_along(): lax.ppermute(value, axis, [(source, source + steps) for source in range(f...  124 us
    psum x1, waiting for transfers between devices, body(): all_states, all_tails = lax.psum((candidate, tail_rows), 'ctx')  77.4 us
    psum x1, blocking collectives, finish(): total_squares = lax.psum(partial_squares, 'tp')  28.6 us
    add x31, other arithmetic, carry_step(): return passed_along(end_decay[:, None, None] * state + end_state, 'ctx', 1)  21.3 us
    all_gather x1, blocking collectives, body(): lax.all_gather(branch_bc, 'tp', axis=0, tiled=True)  17.5 us
  transfers between devices with their start and end apart: 34, of which 32 were waited for; matrix products, arithmetic and copies ran while one was open for 5% of the time, Pallas kernels for 0%

profile of v1, /device:TPU:1, one launch (start us, length us, event | category | flops | bytes accessed | tf_op | source)
XLA Modules:
  0.0 634.7 jit_solution(2501920792919413146)
XLA Ops:
  8.6 11.8 %all-to-all-start = ((bf16[16,16,256]{2,1,0:T(8,128)(2,1)}), bf16[16,16,256]{2,1,0:T(8,128)(2,1)S(1)}, u32[]{:S(2)}, u32[]{:S(2)}) async-start(bf16[16,16,256]{2,1,0:T(8,128)(2,1)} %stack.2), calls=%async_computation | async-start | bytes 262144 | tf_op jit(solution)/shard_map/all_to_all | solution.py:198
  35.8 17.5 %all_gather.3 = bf16[256,256]{1,0:T(8,128)(2,1)S(1)} all-gather(bf16[16,256]{1,0:T(8,128)(2,1)S(1)} %copy-done.29), channel_id=1, replica_groups=mesh['ctx'=32,'tp'=16] {'tp'}, dimensions={0}, use_global_device_ids=true | all-gather | bytes 139264 | tf_op jit(solution)/shard_map/all_gather | solution.py:200
  68.1 304.2 %while.10 = (s32[]{:T(128)}, f32[8,64,128]{2,1,0:T(8,128)S(1)}, f32[8]{0:T(128)}, f32[8,64,128]{2,1,0:T(8,128)S(1)}, s32[]{:T(128)}) while((s32[]{:T(128)}, f32[8,64,128]{2,1,0:T(8,128)S(1)}, f32[8]{0:T(128)}, f32[8,64,128]{2,1,0:T(8,128)S(1)}, s32[]{:T(128)}) %tuple.49), condition=%wide.region_3.4_spmd, body=%wide.region_2.3_spmd.sunk | while | flops 131074 | bytes 1835141 | solution.py:227
  72.1 5.2 collective-permute-done
  78.0 4.1 collective-permute-start
  82.1 4.3 collective-permute-done
  87.1 4.1 collective-permute-start
  91.2 3.3 collective-permute-done
  95.2 4.2 collective-permute-start
  99.4 3.3 collective-permute-done
  103.4 3.8 collective-permute-start
  107.2 3.3 collective-permute-done
  111.2 4.1 collective-permute-start
  115.2 3.3 collective-permute-done
  119.2 5.0 collective-permute-start
  124.3 3.3 collective-permute-done
  128.2 5.0 collective-permute-start
  133.3 3.6 collective-permute-done
  137.6 5.3 collective-permute-start
  142.9 4.7 collective-permute-done
  148.3 5.6 collective-permute-start
  153.9 5.7 collective-permute-done
  160.3 6.0 collective-permute-start
  166.3 5.3 collective-permute-done
  172.2 4.6 collective-permute-start
  176.9 4.0 collective-permute-done
  181.5 4.2 collective-permute-start
  185.7 3.3 collective-permute-done
  189.7 5.3 collective-permute-start
  195.1 3.3 collective-permute-done
  199.0 5.3 collective-permute-start
  204.4 3.3 collective-permute-done
  208.3 5.3 collective-permute-start
  213.7 3.3 collective-permute-done
  217.7 5.0 collective-permute-start
  222.7 3.3 collective-permute-done
  226.7 5.0 collective-permute-start
  231.7 4.0 collective-permute-done
  236.5 5.5 collective-permute-start
  241.9 5.1 collective-permute-done
  247.7 5.0 collective-permute-start
  252.8 5.7 collective-permute-done
  259.2 4.1 collective-permute-start
  263.3 5.6 collective-permute-done
  269.7 4.5 collective-permute-start
  274.2 5.1 collective-permute-done
  280.0 5.6 collective-permute-start
  285.6 5.0 collective-permute-done
  291.3 7.3 %collective-permute-start = (f32[8,64,128]{2,1,0:T(8,128)S(1)}, f32[8,64,128]{2,1,0:T(8,128)S(1)}, u32[]{:S(2)}, u32[]{:S(2)}) collective-permute-start(f32[8,64,128]{2,1,0:T(8,128)S(1)} %multiply_add_fusion.4), channel_id=1, source_target_pairs={{0,16},{16,32},{32,48},{48,64},{64,80},{80,96},{96,112},{112,128},... | collective-permute-start | bytes 786440 | tf_op jit(solution)/shard_map/while/body/eval_jaxpr/ppermute | solution.py:14
  298.6 4.3 collective-permute-done
  303.6 6.0 collective-permute-start
  309.6 3.3 collective-permute-done
  313.6 5.8 collective-permute-start
  323.4 5.1 collective-permute-start
  332.5 5.2 collective-permute-start
  337.7 3.3 collective-permute-done
  341.7 6.2 collective-permute-start
  348.0 3.3 collective-permute-done
  351.9 6.2 collective-permute-start
  362.1 6.2 collective-permute-start
  368.4 4.0 collective-permute-done
  377.9 130.2 %psum.29 = bf16[8,3,768]{2,1,0:T(4,128)(2,1)S(1)} all-reduce(f32[8,3,768]{2,1,0:T(4,128)S(1)} %reshape.514), channel_id=1, replica_groups=mesh['ctx'=32,'tp'=16] {'ctx'}, use_global_device_ids=true, to_apply=%region_14.15 | all-reduce | flops 18432 | bytes 110592 | tf_op jit(solution)/shard_map/psum | solution.py:248
  513.8 77.4 %all-reduce.6.cloned.1.call-done = f32[8,8,64,128]{3,2,1,0:T(8,128)} async-done(((f32[8,8,64,128]{3,2,1,0:T(8,128)}), f32[8,8,64,128]{3,2,1,0:T(8,128)}) %all-reduce.6.cloned.1.call-update) | async-done | bytes 2097168 | tf_op jit(solution)/shard_map/psum | solution.py:248
  597.4 28.6 %all-reduce.3 = (f32[256,1]{0,1:T(1,128)S(1)}, f32[256,1]{0,1:T(1,128)S(1)}) all-reduce(f32[256,1]{0,1:T(1,128)S(1)} %bitcast.104, f32[256,1]{0,1:T(1,128)S(1)} %bitcast.107), channel_id=1, replica_groups=mesh['ctx'=32,'tp'=16] {'tp'}, use_global_device_ids=true, to_apply=%region_5.6 | all-reduce | flops 512 | bytes 4096 | tf_op jit(solution)/shard_map/psum | solution.py:78
  (274 shorter events, 84.1 us)
Async XLA Ops:
  8.6 48.7 %all-to-all-start = ((bf16[16,16,256]{2,1,0:T(8,128)(2,1)}), bf16[16,16,256]{2,1,0:T(8,128)(2,1)S(1)}, u32[]{:S(2)}, u32[]{:S(2)}) async-start(bf16[16,16,256]{2,1,0:T(8,128)(2,1)} %stack.2), calls=%async_computation | async-start | bytes 262144 | tf_op jit(solution)/shard_map/all_to_all | solution.py:198
  20.5 570.7 %all-reduce.6.cloned.1.call-start = ((), (), s32[]{:S(2)}) async-start(), calls=%async_computation.1 | async-start | bytes 4194304 | tf_op jit(solution)/shard_map/psum | solution.py:248
  24.7 32.6 %copy-start = (bf16[256,512]{1,0:T(8,128)(2,1)S(1)}, bf16[256,512]{1,0:T(8,128)(2,1)}, u32[]{:S(2)}) copy-start(bf16[256,512]{1,0:T(8,128)(2,1)} %param.19) | copy-start | bytes 786436
  30.1 34.5 %copy-start.48 = (pred[8]{0:T(512)(128)(4,1)}, pred[8]{0:T(512)(128)(4,1)S(1)}, u32[]{:S(2)}) copy-start(pred[8]{0:T(512)(128)(4,1)S(1)} %get-tuple-element.70) | copy-start | bytes 28
  31.0 33.7 %copy-start.50 = (pred[2]{0:T(512)(128)(4,1)}, pred[2]{0:T(512)(128)(4,1)S(1)}, u32[]{:S(2)}) copy-start(pred[2]{0:T(512)(128)(4,1)S(1)} %compare_and_fusion.6) | copy-start | bytes 10
  32.4 32.3 %copy-start.13 = (f32[768]{0:T(1024)}, f32[768]{0:T(1024)S(1)}, u32[]{:S(2)}) copy-start(f32[768]{0:T(1024)S(1)} %get-tuple-element.28) | copy-start | bytes 9220
  32.4 32.3 %copy-start.15 = (f32[768]{0:T(1024)}, f32[768]{0:T(1024)S(1)}, u32[]{:S(2)}) copy-start(f32[768]{0:T(1024)S(1)} %get-tuple-element.27) | copy-start | bytes 9220
  32.4 32.3 %copy-start.22 = (f32[768]{0:T(1024)}, f32[768]{0:T(1024)S(1)}, u32[]{:S(2)}) copy-start(f32[768]{0:T(1024)S(1)} %get-tuple-element.25) | copy-start | bytes 9220
  32.4 32.3 %copy-start.24 = (f32[768]{0:T(1024)}, f32[768]{0:T(1024)S(1)}, u32[]{:S(2)}) copy-start(f32[768]{0:T(1024)S(1)} %get-tuple-element.26) | copy-start | bytes 9220
  57.4 7.2 %collective-permute-start.1 = (bf16[3,768]{1,0:T(4,128)(2,1)S(1)}, bf16[3,768]{1,0:T(4,128)(2,1)S(1)}, u32[]{:S(2)}, u32[]{:S(2)}) collective-permute-start(bf16[3,768]{1,0:T(4,128)(2,1)S(1)} %fusion.76), channel_id=1, source_target_pairs={{0,16},{16,32},{32,48},{48,64},{64,80},{80,96},{96,112},{112,128},... | collective-permute-start | bytes 13832 | tf_op jit(solution)/shard_map/ppermute | solution.py:14
  68.9 8.4 %collective-permute-start = (f32[8,64,128]{2,1,0:T(8,128)S(1)}, f32[8,64,128]{2,1,0:T(8,128)S(1)}, u32[]{:S(2)}, u32[]{:S(2)}) collective-permute-start(f32[8,64,128]{2,1,0:T(8,128)S(1)} %multiply_add_fusion.4), channel_id=1, source_target_pairs={{0,16},{16,32},{32,48},{48,64},{64,80},{80,96},{96,112},{112,128},... | collective-permute-start | bytes 786440 | tf_op jit(solution)/shard_map/while/body/eval_jaxpr/ppermute | solution.py:14
  78.0 8.4 %collective-permute-start = (f32[8,64,128]{2,1,0:T(8,128)S(1)}, f32[8,64,128]{2,1,0:T(8,128)S(1)}, u32[]{:S(2)}, u32[]{:S(2)}) collective-permute-start(f32[8,64,128]{2,1,0:T(8,128)S(1)} %multiply_add_fusion.4), channel_id=1, source_target_pairs={{0,16},{16,32},{32,48},{48,64},{64,80},{80,96},{96,112},{112,128},... | collective-permute-start | bytes 786440 | tf_op jit(solution)/shard_map/while/body/eval_jaxpr/ppermute | solution.py:14
  87.1 7.4 %collective-permute-start = (f32[8,64,128]{2,1,0:T(8,128)S(1)}, f32[8,64,128]{2,1,0:T(8,128)S(1)}, u32[]{:S(2)}, u32[]{:S(2)}) collective-permute-start(f32[8,64,128]{2,1,0:T(8,128)S(1)} %multiply_add_fusion.4), channel_id=1, source_target_pairs={{0,16},{16,32},{32,48},{48,64},{64,80},{80,96},{96,112},{112,128},... | collective-permute-start | bytes 786440 | tf_op jit(solution)/shard_map/while/body/eval_jaxpr/ppermute | solution.py:14
  95.2 7.5 %collective-permute-start = (f32[8,64,128]{2,1,0:T(8,128)S(1)}, f32[8,64,128]{2,1,0:T(8,128)S(1)}, u32[]{:S(2)}, u32[]{:S(2)}) collective-permute-start(f32[8,64,128]{2,1,0:T(8,128)S(1)} %multiply_add_fusion.4), channel_id=1, source_target_pairs={{0,16},{16,32},{32,48},{48,64},{64,80},{80,96},{96,112},{112,128},... | collective-permute-start | bytes 786440 | tf_op jit(solution)/shard_map/while/body/eval_jaxpr/ppermute | solution.py:14
  103.4 7.1 %collective-permute-start = (f32[8,64,128]{2,1,0:T(8,128)S(1)}, f32[8,64,128]{2,1,0:T(8,128)S(1)}, u32[]{:S(2)}, u32[]{:S(2)}) collective-permute-start(f32[8,64,128]{2,1,0:T(8,128)S(1)} %multiply_add_fusion.4), channel_id=1, source_target_pairs={{0,16},{16,32},{32,48},{48,64},{64,80},{80,96},{96,112},{112,128},... | collective-permute-start | bytes 786440 | tf_op jit(solution)/shard_map/while/body/eval_jaxpr/ppermute | solution.py:14
  111.2 7.4 %collective-permute-start = (f32[8,64,128]{2,1,0:T(8,128)S(1)}, f32[8,64,128]{2,1,0:T(8,128)S(1)}, u32[]{:S(2)}, u32[]{:S(2)}) collective-permute-start(f32[8,64,128]{2,1,0:T(8,128)S(1)} %multiply_add_fusion.4), channel_id=1, source_target_pairs={{0,16},{16,32},{32,48},{48,64},{64,80},{80,96},{96,112},{112,128},... | collective-permute-start | bytes 786440 | tf_op jit(solution)/shard_map/while/body/eval_jaxpr/ppermute | solution.py:14
  119.2 8.3 %collective-permute-start = (f32[8,64,128]{2,1,0:T(8,128)S(1)}, f32[8,64,128]{2,1,0:T(8,128)S(1)}, u32[]{:S(2)}, u32[]{:S(2)}) collective-permute-start(f32[8,64,128]{2,1,0:T(8,128)S(1)} %multiply_add_fusion.4), channel_id=1, source_target_pairs={{0,16},{16,32},{32,48},{48,64},{64,80},{80,96},{96,112},{112,128},... | collective-permute-start | bytes 786440 | tf_op jit(solution)/shard_map/while/body/eval_jaxpr/ppermute | solution.py:14
  128.2 8.6 %collective-permute-start = (f32[8,64,128]{2,1,0:T(8,128)S(1)}, f32[8,64,128]{2,1,0:T(8,128)S(1)}, u32[]{:S(2)}, u32[]{:S(2)}) collective-permute-start(f32[8,64,128]{2,1,0:T(8,128)S(1)} %multiply_add_fusion.4), channel_id=1, source_target_pairs={{0,16},{16,32},{32,48},{48,64},{64,80},{80,96},{96,112},{112,128},... | collective-permute-start | bytes 786440 | tf_op jit(solution)/shard_map/while/body/eval_jaxpr/ppermute | solution.py:14
  137.6 10.0 %collective-permute-start = (f32[8,64,128]{2,1,0:T(8,128)S(1)}, f32[8,64,128]{2,1,0:T(8,128)S(1)}, u32[]{:S(2)}, u32[]{:S(2)}) collective-permute-start(f32[8,64,128]{2,1,0:T(8,128)S(1)} %multiply_add_fusion.4), channel_id=1, source_target_pairs={{0,16},{16,32},{32,48},{48,64},{64,80},{80,96},{96,112},{112,128},... | collective-permute-start | bytes 786440 | tf_op jit(solution)/shard_map/while/body/eval_jaxpr/ppermute | solution.py:14
  148.3 11.3 %collective-permute-start = (f32[8,64,128]{2,1,0:T(8,128)S(1)}, f32[8,64,128]{2,1,0:T(8,128)S(1)}, u32[]{:S(2)}, u32[]{:S(2)}) collective-permute-start(f32[8,64,128]{2,1,0:T(8,128)S(1)} %multiply_add_fusion.4), channel_id=1, source_target_pairs={{0,16},{16,32},{32,48},{48,64},{64,80},{80,96},{96,112},{112,128},... | collective-permute-start | bytes 786440 | tf_op jit(solution)/shard_map/while/body/eval_jaxpr/ppermute | solution.py:14
  160.3 11.2 %collective-permute-start = (f32[8,64,128]{2,1,0:T(8,128)S(1)}, f32[8,64,128]{2,1,0:T(8,128)S(1)}, u32[]{:S(2)}, u32[]{:S(2)}) collective-permute-start(f32[8,64,128]{2,1,0:T(8,128)S(1)} %multiply_add_fusion.4), channel_id=1, source_target_pairs={{0,16},{16,32},{32,48},{48,64},{64,80},{80,96},{96,112},{112,128},... | collective-permute-start | bytes 786440 | tf_op jit(solution)/shard_map/while/body/eval_jaxpr/ppermute | solution.py:14
  172.2 8.6 %collective-permute-start = (f32[8,64,128]{2,1,0:T(8,128)S(1)}, f32[8,64,128]{2,1,0:T(8,128)S(1)}, u32[]{:S(2)}, u32[]{:S(2)}) collective-permute-start(f32[8,64,128]{2,1,0:T(8,128)S(1)} %multiply_add_fusion.4), channel_id=1, source_target_pairs={{0,16},{16,32},{32,48},{48,64},{64,80},{80,96},{96,112},{112,128},... | collective-permute-start | bytes 786440 | tf_op jit(solution)/shard_map/while/body/eval_jaxpr/ppermute | solution.py:14
  181.5 7.5 %collective-permute-start = (f32[8,64,128]{2,1,0:T(8,128)S(1)}, f32[8,64,128]{2,1,0:T(8,128)S(1)}, u32[]{:S(2)}, u32[]{:S(2)}) collective-permute-start(f32[8,64,128]{2,1,0:T(8,128)S(1)} %multiply_add_fusion.4), channel_id=1, source_target_pairs={{0,16},{16,32},{32,48},{48,64},{64,80},{80,96},{96,112},{112,128},... | collective-permute-start | bytes 786440 | tf_op jit(solution)/shard_map/while/body/eval_jaxpr/ppermute | solution.py:14
  189.7 8.6 %collective-permute-start = (f32[8,64,128]{2,1,0:T(8,128)S(1)}, f32[8,64,128]{2,1,0:T(8,128)S(1)}, u32[]{:S(2)}, u32[]{:S(2)}) collective-permute-start(f32[8,64,128]{2,1,0:T(8,128)S(1)} %multiply_add_fusion.4), channel_id=1, source_target_pairs={{0,16},{16,32},{32,48},{48,64},{64,80},{80,96},{96,112},{112,128},... | collective-permute-start | bytes 786440 | tf_op jit(solution)/shard_map/while/body/eval_jaxpr/ppermute | solution.py:14
  199.0 8.6 %collective-permute-start = (f32[8,64,128]{2,1,0:T(8,128)S(1)}, f32[8,64,128]{2,1,0:T(8,128)S(1)}, u32[]{:S(2)}, u32[]{:S(2)}) collective-permute-start(f32[8,64,128]{2,1,0:T(8,128)S(1)} %multiply_add_fusion.4), channel_id=1, source_target_pairs={{0,16},{16,32},{32,48},{48,64},{64,80},{80,96},{96,112},{112,128},... | collective-permute-start | bytes 786440 | tf_op jit(solution)/shard_map/while/body/eval_jaxpr/ppermute | solution.py:14
  208.3 8.6 %collective-permute-start = (f32[8,64,128]{2,1,0:T(8,128)S(1)}, f32[8,64,128]{2,1,0:T(8,128)S(1)}, u32[]{:S(2)}, u32[]{:S(2)}) collective-permute-start(f32[8,64,128]{2,1,0:T(8,128)S(1)} %multiply_add_fusion.4), channel_id=1, source_target_pairs={{0,16},{16,32},{32,48},{48,64},{64,80},{80,96},{96,112},{112,128},... | collective-permute-start | bytes 786440 | tf_op jit(solution)/shard_map/while/body/eval_jaxpr/ppermute | solution.py:14
  217.7 8.3 %collective-permute-start = (f32[8,64,128]{2,1,0:T(8,128)S(1)}, f32[8,64,128]{2,1,0:T(8,128)S(1)}, u32[]{:S(2)}, u32[]{:S(2)}) collective-permute-start(f32[8,64,128]{2,1,0:T(8,128)S(1)} %multiply_add_fusion.4), channel_id=1, source_target_pairs={{0,16},{16,32},{32,48},{48,64},{64,80},{80,96},{96,112},{112,128},... | collective-permute-start | bytes 786440 | tf_op jit(solution)/shard_map/while/body/eval_jaxpr/ppermute | solution.py:14
  226.7 9.1 %collective-permute-start = (f32[8,64,128]{2,1,0:T(8,128)S(1)}, f32[8,64,128]{2,1,0:T(8,128)S(1)}, u32[]{:S(2)}, u32[]{:S(2)}) collective-permute-start(f32[8,64,128]{2,1,0:T(8,128)S(1)} %multiply_add_fusion.4), channel_id=1, source_target_pairs={{0,16},{16,32},{32,48},{48,64},{64,80},{80,96},{96,112},{112,128},... | collective-permute-start | bytes 786440 | tf_op jit(solution)/shard_map/while/body/eval_jaxpr/ppermute | solution.py:14
  236.5 10.5 %collective-permute-start = (f32[8,64,128]{2,1,0:T(8,128)S(1)}, f32[8,64,128]{2,1,0:T(8,128)S(1)}, u32[]{:S(2)}, u32[]{:S(2)}) collective-permute-start(f32[8,64,128]{2,1,0:T(8,128)S(1)} %multiply_add_fusion.4), channel_id=1, source_target_pairs={{0,16},{16,32},{32,48},{48,64},{64,80},{80,96},{96,112},{112,128},... | collective-permute-start | bytes 786440 | tf_op jit(solution)/shard_map/while/body/eval_jaxpr/ppermute | solution.py:14
  247.7 10.8 %collective-permute-start = (f32[8,64,128]{2,1,0:T(8,128)S(1)}, f32[8,64,128]{2,1,0:T(8,128)S(1)}, u32[]{:S(2)}, u32[]{:S(2)}) collective-permute-start(f32[8,64,128]{2,1,0:T(8,128)S(1)} %multiply_add_fusion.4), channel_id=1, source_target_pairs={{0,16},{16,32},{32,48},{48,64},{64,80},{80,96},{96,112},{112,128},... | collective-permute-start | bytes 786440 | tf_op jit(solution)/shard_map/while/body/eval_jaxpr/ppermute | solution.py:14
  259.2 9.8 %collective-permute-start = (f32[8,64,128]{2,1,0:T(8,128)S(1)}, f32[8,64,128]{2,1,0:T(8,128)S(1)}, u32[]{:S(2)}, u32[]{:S(2)}) collective-permute-start(f32[8,64,128]{2,1,0:T(8,128)S(1)} %multiply_add_fusion.4), channel_id=1, source_target_pairs={{0,16},{16,32},{32,48},{48,64},{64,80},{80,96},{96,112},{112,128},... | collective-permute-start | bytes 786440 | tf_op jit(solution)/shard_map/while/body/eval_jaxpr/ppermute | solution.py:14
  269.7 9.6 %collective-permute-start = (f32[8,64,128]{2,1,0:T(8,128)S(1)}, f32[8,64,128]{2,1,0:T(8,128)S(1)}, u32[]{:S(2)}, u32[]{:S(2)}) collective-permute-start(f32[8,64,128]{2,1,0:T(8,128)S(1)} %multiply_add_fusion.4), channel_id=1, source_target_pairs={{0,16},{16,32},{32,48},{48,64},{64,80},{80,96},{96,112},{112,128},... | collective-permute-start | bytes 786440 | tf_op jit(solution)/shard_map/while/body/eval_jaxpr/ppermute | solution.py:14
  280.0 10.6 %collective-permute-start = (f32[8,64,128]{2,1,0:T(8,128)S(1)}, f32[8,64,128]{2,1,0:T(8,128)S(1)}, u32[]{:S(2)}, u32[]{:S(2)}) collective-permute-start(f32[8,64,128]{2,1,0:T(8,128)S(1)} %multiply_add_fusion.4), channel_id=1, source_target_pairs={{0,16},{16,32},{32,48},{48,64},{64,80},{80,96},{96,112},{112,128},... | collective-permute-start | bytes 786440 | tf_op jit(solution)/shard_map/while/body/eval_jaxpr/ppermute | solution.py:14
  291.3 11.6 %collective-permute-start = (f32[8,64,128]{2,1,0:T(8,128)S(1)}, f32[8,64,128]{2,1,0:T(8,128)S(1)}, u32[]{:S(2)}, u32[]{:S(2)}) collective-permute-start(f32[8,64,128]{2,1,0:T(8,128)S(1)} %multiply_add_fusion.4), channel_id=1, source_target_pairs={{0,16},{16,32},{32,48},{48,64},{64,80},{80,96},{96,112},{112,128},... | collective-permute-start | bytes 786440 | tf_op jit(solution)/shard_map/while/body/eval_jaxpr/ppermute | solution.py:14
  303.6 9.3 %collective-permute-start = (f32[8,64,128]{2,1,0:T(8,128)S(1)}, f32[8,64,128]{2,1,0:T(8,128)S(1)}, u32[]{:S(2)}, u32[]{:S(2)}) collective-permute-start(f32[8,64,128]{2,1,0:T(8,128)S(1)} %multiply_add_fusion.4), channel_id=1, source_target_pairs={{0,16},{16,32},{32,48},{48,64},{64,80},{80,96},{96,112},{112,128},... | collective-permute-start | bytes 786440 | tf_op jit(solution)/shard_map/while/body/eval_jaxpr/ppermute | solution.py:14
  313.6 9.1 %collective-permute-start = (f32[8,64,128]{2,1,0:T(8,128)S(1)}, f32[8,64,128]{2,1,0:T(8,128)S(1)}, u32[]{:S(2)}, u32[]{:S(2)}) collective-permute-start(f32[8,64,128]{2,1,0:T(8,128)S(1)} %multiply_add_fusion.4), channel_id=1, source_target_pairs={{0,16},{16,32},{32,48},{48,64},{64,80},{80,96},{96,112},{112,128},... | collective-permute-start | bytes 786440 | tf_op jit(solution)/shard_map/while/body/eval_jaxpr/ppermute | solution.py:14
  323.4 8.4 %collective-permute-start = (f32[8,64,128]{2,1,0:T(8,128)S(1)}, f32[8,64,128]{2,1,0:T(8,128)S(1)}, u32[]{:S(2)}, u32[]{:S(2)}) collective-permute-start(f32[8,64,128]{2,1,0:T(8,128)S(1)} %multiply_add_fusion.4), channel_id=1, source_target_pairs={{0,16},{16,32},{32,48},{48,64},{64,80},{80,96},{96,112},{112,128},... | collective-permute-start | bytes 786440 | tf_op jit(solution)/shard_map/while/body/eval_jaxpr/ppermute | solution.py:14
  332.5 8.5 %collective-permute-start = (f32[8,64,128]{2,1,0:T(8,128)S(1)}, f32[8,64,128]{2,1,0:T(8,128)S(1)}, u32[]{:S(2)}, u32[]{:S(2)}) collective-permute-start(f32[8,64,128]{2,1,0:T(8,128)S(1)} %multiply_add_fusion.4), channel_id=1, source_target_pairs={{0,16},{16,32},{32,48},{48,64},{64,80},{80,96},{96,112},{112,128},... | collective-permute-start | bytes 786440 | tf_op jit(solution)/shard_map/while/body/eval_jaxpr/ppermute | solution.py:14
  341.7 9.5 %collective-permute-start = (f32[8,64,128]{2,1,0:T(8,128)S(1)}, f32[8,64,128]{2,1,0:T(8,128)S(1)}, u32[]{:S(2)}, u32[]{:S(2)}) collective-permute-start(f32[8,64,128]{2,1,0:T(8,128)S(1)} %multiply_add_fusion.4), channel_id=1, source_target_pairs={{0,16},{16,32},{32,48},{48,64},{64,80},{80,96},{96,112},{112,128},... | collective-permute-start | bytes 786440 | tf_op jit(solution)/shard_map/while/body/eval_jaxpr/ppermute | solution.py:14
  351.9 9.5 %collective-permute-start = (f32[8,64,128]{2,1,0:T(8,128)S(1)}, f32[8,64,128]{2,1,0:T(8,128)S(1)}, u32[]{:S(2)}, u32[]{:S(2)}) collective-permute-start(f32[8,64,128]{2,1,0:T(8,128)S(1)} %multiply_add_fusion.4), channel_id=1, source_target_pairs={{0,16},{16,32},{32,48},{48,64},{64,80},{80,96},{96,112},{112,128},... | collective-permute-start | bytes 786440 | tf_op jit(solution)/shard_map/while/body/eval_jaxpr/ppermute | solution.py:14
  362.1 10.2 %collective-permute-start = (f32[8,64,128]{2,1,0:T(8,128)S(1)}, f32[8,64,128]{2,1,0:T(8,128)S(1)}, u32[]{:S(2)}, u32[]{:S(2)}) collective-permute-start(f32[8,64,128]{2,1,0:T(8,128)S(1)} %multiply_add_fusion.4), channel_id=1, source_target_pairs={{0,16},{16,32},{32,48},{48,64},{64,80},{80,96},{96,112},{112,128},... | collective-permute-start | bytes 786440 | tf_op jit(solution)/shard_map/while/body/eval_jaxpr/ppermute | solution.py:14
  377.1 131.7 %copy-start.16 = (f32[768]{0:T(1024)S(1)}, f32[768]{0:T(1024)}, u32[]{:S(2)}) copy-start(f32[768]{0:T(1024)} %copy-done.15) | copy-start | bytes 9220
  377.1 131.7 %copy-start.21 = (s32[256]{0:T(256)S(1)}, s32[256]{0:T(256)}, u32[]{:S(2)}) copy-start(s32[256]{0:T(256)} %copy-done.20) | copy-start | bytes 3076
  377.2 131.7 %copy-start.37 = (s32[256]{0:T(256)S(1)}, s32[256]{0:T(256)}, u32[]{:S(2)}) copy-start(s32[256]{0:T(256)} %get-tuple-element.66) | copy-start | bytes 3076
  377.2 131.7 %copy-start.38 = (s32[6]{0:T(128)S(1)}, s32[6]{0:T(128)}, u32[]{:S(2)}) copy-start(s32[6]{0:T(128)} %get-tuple-element.73) | copy-start | bytes 76
  377.2 131.7 %copy-start.39 = (s32[6]{0:T(128)S(1)}, s32[6]{0:T(128)}, u32[]{:S(2)}) copy-start(s32[6]{0:T(128)} %get-tuple-element.74) | copy-start | bytes 76
  377.2 131.7 %copy-start.40 = (pred[6]{0:T(512)(128)(4,1)S(1)}, pred[6]{0:T(512)(128)(4,1)}, u32[]{:S(2)}) copy-start(pred[6]{0:T(512)(128)(4,1)} %broadcast_in_dim.287) | copy-start | bytes 22
  377.2 131.7 %copy-start.43 = (pred[256]{0:T(512)(128)(4,1)S(1)}, pred[256]{0:T(512)(128)(4,1)}, u32[]{:S(2)}) copy-start(pred[256]{0:T(512)(128)(4,1)} %get-tuple-element.61) | copy-start | bytes 772
  377.2 131.7 %copy-start.44 = (pred[256]{0:T(512)(128)(4,1)S(1)}, pred[256]{0:T(512)(128)(4,1)}, u32[]{:S(2)}) copy-start(pred[256]{0:T(512)(128)(4,1)} %get-tuple-element.62) | copy-start | bytes 772
  377.2 132.1 %copy-start.14 = (f32[768]{0:T(1024)S(1)}, f32[768]{0:T(1024)}, u32[]{:S(2)}) copy-start(f32[768]{0:T(1024)} %copy-done.13) | copy-start | bytes 9220
  377.2 132.1 %copy-start.36 = (s32[256]{0:T(256)S(1)}, s32[256]{0:T(256)}, u32[]{:S(2)}) copy-start(s32[256]{0:T(256)} %get-tuple-element.65) | copy-start | bytes 3076
  377.2 132.1 %copy-start.41 = (pred[256]{0:T(512)(128)(4,1)S(1)}, pred[256]{0:T(512)(128)(4,1)}, u32[]{:S(2)}) copy-start(pred[256]{0:T(512)(128)(4,1)} %get-tuple-element.59) | copy-start | bytes 772
  377.2 132.1 %copy-start.42 = (pred[256]{0:T(512)(128)(4,1)S(1)}, pred[256]{0:T(512)(128)(4,1)}, u32[]{:S(2)}) copy-start(pred[256]{0:T(512)(128)(4,1)} %get-tuple-element.60) | copy-start | bytes 772
  377.5 132.3 %copy-start.23 = (f32[768]{0:T(1024)S(1)}, f32[768]{0:T(1024)}, u32[]{:S(2)}) copy-start(f32[768]{0:T(1024)} %copy-done.22) | copy-start | bytes 9220
  377.5 132.3 %copy-start.25 = (f32[768]{0:T(1024)S(1)}, f32[768]{0:T(1024)}, u32[]{:S(2)}) copy-start(f32[768]{0:T(1024)} %copy-done.24) | copy-start | bytes 9220
  377.5 132.3 %copy-start.49 = (s32[256]{0:T(256)S(1)}, s32[256]{0:T(256)}, u32[]{:S(2)}) copy-start(s32[256]{0:T(256)} %get-tuple-element.64) | copy-start | bytes 3076
  377.5 132.3 %copy-start.53 = (pred[256]{0:T(512)(128)(4,1)S(1)}, pred[256]{0:T(512)(128)(4,1)}, u32[]{:S(2)}) copy-start(pred[256]{0:T(512)(128)(4,1)} %get-tuple-element.57) | copy-start | bytes 772
  377.6 132.3 %copy-start.54 = (pred[256]{0:T(512)(128)(4,1)S(1)}, pred[256]{0:T(512)(128)(4,1)}, u32[]{:S(2)}) copy-start(pred[256]{0:T(512)(128)(4,1)} %get-tuple-element.58) | copy-start | bytes 772
  511.3 82.2 %copy-start.51 = (pred[2]{0:T(512)(128)(4,1)S(1)}, pred[2]{0:T(512)(128)(4,1)}, u32[]{:S(2)}) copy-start(pred[2]{0:T(512)(128)(4,1)} %copy-done.50) | copy-start | bytes 10
  511.3 82.3 %copy-start.52 = (pred[256]{0:T(512)(128)(4,1)S(1)}, pred[256]{0:T(512)(128)(4,1)}, u32[]{:S(2)}) copy-start(pred[256]{0:T(512)(128)(4,1)} %broadcast_compare_fusion.2) | copy-start | bytes 772
  512.4 82.4 %copy-start.45 = (pred[256]{0:T(512)(128)(4,1)S(1)}, pred[256]{0:T(512)(128)(4,1)}, u32[]{:S(2)}) copy-start(pred[256]{0:T(512)(128)(4,1)} %get-tuple-element.45) | copy-start | bytes 772
  512.7 83.4 %copy-start.12 = (pred[256,256]{1,0:T(8,128)(4,1)S(1)}, pred[256,256]{1,0:T(8,128)(4,1)}, u32[]{:S(2)}) copy-start(pred[256,256]{1,0:T(8,128)(4,1)} %and_and_fusion) | copy-start | bytes 196612
  512.7 83.4 %copy-start.19 = (f32[8,256]{1,0:T(8,128)S(1)}, f32[8,256]{1,0:T(8,128)}, u32[]{:S(2)}) copy-start(f32[8,256]{1,0:T(8,128)} %copy-done.18) | copy-start | bytes 24580
  512.7 83.4 %copy-start.30 = (f32[8,256]{1,0:T(8,128)S(1)}, f32[8,256]{1,0:T(8,128)}, u32[]{:S(2)}) copy-start(f32[8,256]{1,0:T(8,128)} %copy.135) | copy-start | bytes 24580
  (29 other events, 337.8 us)
Sparse Core Ops, SparseCore 0:
  374.9 216.2 all-reduce.5
